TPU v7x, 256 devices: a whole 4x4x8 slice. The times are simulated.
256 devices in a mesh: dp: 64 (over x, z, core), tensor: 4 (over y).
Axes of the slice: x: 4, y: 4, z: 8, core: 2. Of those that a mesh axis runs over, the one named last changes fastest.
Arguments:
- tokens: bfloat16 [131072, 2560], P('dp'), may hold values from -6 to 6
- upstream: bfloat16 [131072, 2560], P('dp', 'tensor'), may hold values from -0.19921875 to 0.19921875
- memory: bfloat16 [64, 2560, 2560], P('dp', None, 'tensor'), may hold values from -3 to 3
- block_lists: int32 [64, 4, 1024], P('dp', 'tensor'), may hold values from 0 to 12799, as said below
- leader: int32 [1], replicated, may hold values from 0 to 63
Outputs:
- summed: float32 [4, 1024, 128], P('tensor')
- memory_out: bfloat16 [64, 2560, 2560], P('dp', None, 'tensor')
Inputs may be any that keep to these rules, and one draw needn't show every extreme that they name: `block_lists`: each row lists 1024 distinct block numbers in increasing order, always including 0 and 12799.
All inputs are finite; a program needn't handle non-finite values.
Results may differ from a plain program's by a relative error of at most 0.001.
Values sent between devices are 32-bit elements; how exact they have to be, the bound alone decides.
A program may use at most 128 MiB of HBM per device.

v0:
```python
import jax
import jax.numpy as jnp
from jax import lax
from jax.sharding import PartitionSpec as P

HD = 128


LOWPASS = 0.3


def broadcast(value, axis, source):
    kept = jnp.where(lax.axis_index(axis) == source, value, 0).astype(value.dtype)
    return lax.psum(kept, axis)


def body(tokens, upstream, memory, block_lists, leader):
    columns = upstream.shape[1]
    features = tokens.shape[1]
    heads_here = columns // HD
    chosen = broadcast(block_lists[0, 0], "dp", leader[0])
    stored = memory[0].astype(jnp.float32)
    gradient = lax.dot_general(
        tokens, upstream, (((0,), (0,)), ((), ())), preferred_element_type=jnp.float32
    )
    blocks = (gradient + stored).reshape(features * heads_here, HD)
    packed = jnp.take(blocks, chosen, axis=0)
    owned = lax.psum_scatter(packed, "dp", scatter_dimension=0, tiled=True)
    summed = lax.all_gather(owned, "dp", axis=0, tiled=True)
    unsent = 1.0 - jnp.zeros((features * heads_here,), jnp.float32).at[chosen].set(1.0)
    error = (blocks * unsent[:, None]).reshape(features, columns)
    updated = ((1.0 - LOWPASS) * stored + LOWPASS * error).astype(jnp.bfloat16)
    return (summed[None], updated[None])


def solution(mesh):
    placed = (
        P("dp", None),
        P("dp", "tensor"),
        P("dp", None, "tensor"),
        P("dp", "tensor", None),
        P(),
    )
    return jax.shard_map(
        body,
        mesh=mesh,
        in_specs=placed,
        out_specs=(P("tensor", None, None), P("dp", None, "tensor")),
        check_vma=False,
    )
```

profile of v0, /device:TPU:1, one launch (start us, length us, event | category | flops | bytes accessed | tf_op | source)
XLA Modules:
  0.0 251.5 jit_solution(2816615629257744543)
XLA Ops:
  7.2 0.0 copy-start
  7.2 0.0 reduce-scatter.2.cloned.1.call-start
  8.0 20.7 %psum.7 = s32[1024]{0:T(1024)S(1)} all-reduce(s32[1024]{0:T(1024)S(1)} %bitcast.16), channel_id=1, replica_groups=mesh['dp'=64,'tensor'=4] {'dp'}, use_global_device_ids=true, to_apply=%region_0.1 | all-reduce | flops 1024 | bytes 8192 | tf_op jit(solution)/shard_map/psum | solution.py:14
  28.8 0.0 copy-done
  28.8 13.3 %convert_add_fusion = f32[2560,640]{1,0:T(8,128)} fusion(bf16[2048,2560]{1,0:T(8,128)(2,1)} %param.5, bf16[2048,640]{1,0:T(8,128)(2,1)S(1)} %copy-done, bf16[1,2560,640]{2,1,0:T(8,128)(2,1)} %param.7), kind=kOutput, calls=%fused_computation.3 | convolution fusion | flops 6714163200 | bytes 22937600 | tf_op jit(solution)/shard_map/dot_general | solution.py:23
  42.1 7.4 %reshape.22 = f32[12800,128]{1,0:T(8,128)} reshape(f32[2560,640]{1,0:T(8,128)} %convert_add_fusion) | data formatting | bytes 13107200 | tf_op jit(solution)/shard_map/reshape | solution.py:26
  49.5 5.7 %gather_fusion = f32[1024,128]{1,0:T(8,128)S(1)} fusion(f32[12800,128]{1,0:T(8,128)} %reshape.22, s32[1024]{0:T(1024)S(1)} %get-tuple-element.3), kind=kCustom, calls=%fused_computation | custom fusion | bytes 1052672 | tf_op jit(solution)/shard_map/jit(_take)/gather | solution.py:27
  55.2 1.0 broadcast_select_fusion
  56.2 0.0 reduce-scatter.2.cloned.1.call-update
  56.2 4.3 %scatter_custom_fusion = f32[12800]{0:T(1024)S(1)} fusion(s32[1024]{0:T(1024)S(1)} %get-tuple-element.2, f32[1024]{0:T(1024)S(1)} %broadcast.8, f32[]{:T(128)} %constant.32.clone.1), kind=kCustom, calls=%fused_computation.8 | custom fusion | bytes 51204 | tf_op jit(solution)/shard_map/scatter | solution.py:30
  60.6 2.3 mul.27
  62.9 1.7 copy.7
  64.6 3.5 %mul.28 = f32[2560,5,128]{0,2,1:T(8,128)} broadcast(f32[2560,5]{0,1:T(8,128)S(1)} %copy.7), dimensions={0,1} | broadcast | bytes 6604800 | tf_op jit(solution)/shard_map/mul | solution.py:31
  68.1 8.2 %copy.8 = f32[2560,640]{1,0:T(8,128)} copy(f32[2560,640]{0,1:T(8,128)} %bitcast.14) | data formatting | bytes 13107200 | tf_op jit(solution)/shard_map/mul | solution.py:31
  76.3 8.7 %fusion.2 = bf16[1,2560,640]{2,1,0:T(8,128)(2,1)} fusion(f32[2560,640]{1,0:T(8,128)} %convert_add_fusion, f32[2560,640]{1,0:T(8,128)} %copy.8, bf16[1,2560,640]{2,1,0:T(8,128)(2,1)} %param.7), kind=kLoop, calls=%fused_computation.6 | loop fusion | flops 9830400 | bytes 19660800 | tf_op jit(solution)/shard_map/broadcast_in_dim | solution.py:33
  85.0 104.2 %reduce-scatter.2.cloned.1.call-done = f32[16,128]{1,0:T(8,128)} async-done(((f32[1024,128]{1,0:T(8,128)}), f32[16,128]{1,0:T(8,128)}) %reduce-scatter.2.cloned.1.call-update) | async-done | bytes 8208 | tf_op jit(solution)/shard_map/reduce_scatter | solution.py:28
  189.2 54.7 %all_gather.3 = f32[1024,128]{1,0:T(8,128)S(1)} all-gather(f32[16,128]{1,0:T(8,128)} %reduce-scatter.2.cloned.1.call-done), channel_id=1, replica_groups=mesh['dp'=64,'tensor'=4] {'dp'}, dimensions={0}, use_global_device_ids=true | all-gather | bytes 532480 | tf_op jit(solution)/shard_map/all_gather | solution.py:29
  243.9 0.8 copy.11
  (5 shorter events, 0.0 us)
Async XLA Ops:
  7.2 21.6 %copy-start = (bf16[2048,640]{1,0:T(8,128)(2,1)S(1)}, bf16[2048,640]{1,0:T(8,128)(2,1)}, u32[]{:S(2)}) copy-start(bf16[2048,640]{1,0:T(8,128)(2,1)} %param.6) | copy-start | bytes 7864324
  7.2 182.0 %reduce-scatter.2.cloned.1.call-start = ((), (), s32[]{:S(2)}) async-start(), calls=%async_computation.1 | async-start | bytes 532480 | tf_op jit(solution)/shard_map/reduce_scatter | solution.py:28
Sparse Core Ops, SparseCore 0:
  56.3 132.8 reduce-scatter.1
where the time goes:
time: 252 us
  waiting for transfers between devices  104 us (41%)
  blocking collectives  75.4 us (30%)
  local copies, waits for them, and re-layouts  33.9 us (13%)
  between operations  14.9 us (6%)
  matrix products  13.3 us (5%)
  other arithmetic  9.75 us (4%)
    reduce_scatter x1, waiting for transfers between devices, body(): owned = lax.psum_scatter(packed, 'dp', scatter_dimension=0, tiled=True)  104 us
    all_gather x1, blocking collectives, body(): summed = lax.all_gather(owned, 'dp', axis=0, tiled=True)  54.7 us
    psum x1, blocking collectives, broadcast(): return lax.psum(kept, axis)  20.7 us
    mul x4, local copies, waits for them, and re-layouts, body(): error = (blocks * unsent[:, None]).reshape(features, columns)  15.7 us
    dot_general x1, matrix products, body(): lax.dot_general(tokens, upstream, (((0,), (0,)), ((), ())), preferred_ele...  13.3 us
    broadcast_in_dim x1, other arithmetic, body(): return (summed[None], updated[None])  8.71 us
    reshape x1, local copies, waits for them, and re-layouts, body(): blocks = (gradient + stored).reshape(features * heads_here, HD)  7.39 us
    gather x1, local copies, waits for them, and re-layouts, body(): packed = jnp.take(blocks, chosen, axis=0)  5.66 us
  transfers between devices with their start and end apart: 1, of which 1 were waited for; matrix products, arithmetic and copies ran while one was open for 11% of the time, Pallas kernels for 0%

commit v1 on v0

v1 whole, which is shorter than its diff:
```python
import functools

import jax
import jax.numpy as jnp
from jax import lax
from jax.experimental import pallas as pl
from jax.experimental.pallas import tpu as pltpu
from jax.sharding import PartitionSpec as P

HD = 128
LOWPASS = 0.3
NX, NZ = 4, 8
F32, BF16, I32 = jnp.float32, jnp.bfloat16, jnp.int32
MESH = pl.DeviceIdType.MESH


def dot(a, b, ca, cb):
    return lax.dot_general(a, b, (((ca,), (cb,)), ((), ())), preferred_element_type=F32)


def kernel(
    tokens, upstream, memory, lists, leader, summed, updated,
    tok, up, up_t, mem, grad_t, blocks, heads, lone, ltwo, lthree, rows_at, heads_at, index_v, index_s,
    peer_part, own_part, from_core, from_x, from_z, part,
    load_sem, index_sem, send_sem, recv_sem,
):
    features = tokens.shape[1]
    columns = upstream.shape[1]
    heads_here = columns // HD
    chosen = lists.shape[1]
    half, quarter, share = chosen // 2, chosen // 2 // NX, chosen // 2 // NX // NZ
    width = grad_t.shape[2]
    chunks = features // width

    me = lax.axis_index("dp")
    core = lax.rem(me, 2)
    z = lax.rem(me // 2, NZ)
    x = me // (2 * NZ)
    other = {"dp": me + 1 - 2 * core}

    def x_peer(step):
        return {"dp": (lax.rem(x + step, NX) * NZ + z) * 2 + core}

    def z_peer(step):
        return {"dp": (x * NZ + lax.rem(z + step, NZ)) * 2 + core}

    def remote(src, dst, at, device):
        return pltpu.make_async_remote_copy(
            src_ref=src, dst_ref=dst, send_sem=send_sem.at[at], recv_sem=recv_sem.at[at],
            device_id=device, device_id_type=MESH,
        )

    L1, L2, L3, C, X, Z, ZG, XG, CG = 0, 1, 4, 11, 15, 18, 25, 32, 35

    barrier = pltpu.get_barrier_semaphore()
    partners = [other] + [x_peer(d) for d in range(1, NX)] + [z_peer(e) for e in range(1, NZ)]
    for partner in partners:
        pl.semaphore_signal(barrier, inc=1, device_id=partner, device_id_type=MESH)

    load_up = pltpu.make_async_copy(upstream, up, load_sem.at[0])
    load_up.start()
    loads = []
    for i in range(chunks):
        at = pl.ds(i * width, width)
        load = pltpu.make_async_copy(tokens.at[:, at], tok.at[:, at], load_sem.at[1 + 2 * i])
        load.start()
        keep = pltpu.make_async_copy(memory.at[0, at], mem.at[at], load_sem.at[2 + 2 * i])
        keep.start()
        loads.append((load, keep))

    block = lists[...]
    row = lax.shift_right_logical(block * 52429, 18)
    code = (block - row * heads_here) * 4096 + row
    lone[...] = code * jnp.where(leader[0] == me, 1, 0)

    load_up.wait()
    piece = 512
    for j in range(up.shape[0] // piece):
        up_t[:, j * piece : (j + 1) * piece] = up[j * piece : (j + 1) * piece, :].T

    def finish(i):
        grad = grad_t[i % 2].T
        stored = mem[i * width : (i + 1) * width, :].astype(F32)
        for h in range(heads_here):
            cols = slice(h * HD, (h + 1) * HD)
            blocks[pl.ds(h * features + i * width, width), :] = grad[:, cols] + stored[:, cols]

    first = remote(lone, ltwo.at[0], L1, other)
    second = [remote(lone, ltwo.at[d], L2 + d - 1, x_peer(d)) for d in range(1, NX)]
    third = [remote(lone, lthree.at[e - 1], L3 + e - 1, z_peer(e)) for e in range(1, NZ)]
    index_copy = pltpu.make_async_copy(index_v, index_s, index_sem)

    for i in range(chunks):
        if i == 1:
            pl.semaphore_wait(barrier, len(partners))
            first.start()
        if i == 2:
            first.wait()
            lone[...] = lone[...] + ltwo[0]
            for copy in second:
                copy.start()
        if i == 3:
            for copy in second:
                copy.wait()
            lone[...] = lone[...] + (ltwo[1] + ltwo[2] + ltwo[3])
            for copy in third:
                copy.start()
        if i == 4:
            for copy in third:
                copy.wait()
            total = lone[...]
            for e in range(NZ - 1):
                total = total + lthree[e]
            head = lax.shift_right_logical(total, 12)
            row = total - head * 4096
            rows_at[...] = row
            heads_at[...] = head
            index_v[...] = head * features + row
            index_copy.start()
        for load in loads[i]:
            load.wait()
        grad_t[i % 2] = dot(up_t[...], tok[:, i * width : (i + 1) * width], 1, 0)
        if i > 0:
            finish(i - 1)
    finish(chunks - 1)
    index_copy.wait()

    def gather(target, slot, start):
        unroll = 16

        @pl.loop(0, quarter // unroll)
        def _(step):
            base = pl.multiple_of(step * unroll, unroll)
            for u in range(unroll):
                at = index_s[0, start + base + u]
                target[slot, pl.ds(base + u, 1), :] = blocks[pl.ds(at, 1), :]

    order = [1, 2, 3, 0]
    to_core = [remote(peer_part.at[d], from_core.at[d], C + d, other) for d in range(NX)]
    for d in order:
        gather(peer_part, d, (1 - core) * half + lax.rem(x + d, NX) * quarter)
        to_core[d].start()
    to_x = [None] + [remote(own_part.at[d], from_x.at[d - 1], X + d - 1, x_peer(d)) for d in range(1, NX)]
    for d in order:
        gather(own_part, d, core * half + lax.rem(x + d, NX) * quarter)
        to_core[d].wait_recv()
        own_part[d] = own_part[d] + from_core[d]
        if d:
            to_x[d].start()

    head_row = lax.broadcasted_iota(I32, (columns, 1), 0) // HD
    heads[...] = jnp.where(head_row == heads_at[...], 1.0, 0.0).astype(BF16)

    size = 256

    def update(i):
        at = slice(i * size, (i + 1) * size)
        feature = lax.broadcasted_iota(I32, (size, 1), 0) + i * size
        hit = jnp.where(feature == rows_at[...], 1.0, 0.0).astype(BF16)
        unsent = 1.0 - dot(hit, heads[...], 1, 1)
        for h in range(heads_here):
            cols = slice(h * HD, (h + 1) * HD)
            error = blocks[pl.ds(h * features + i * size, size), :] * unsent[:, cols]
            stored = mem[at, cols].astype(F32)
            updated[0, at, cols] = ((1.0 - LOWPASS) * stored + LOWPASS * error).astype(BF16)

    for i in range(0, 3):
        update(i)

    for d in range(1, NX):
        to_x[d].wait_recv()
    part[...] = own_part[0] + (from_x[0] + from_x[1] + from_x[2])
    to_z = [
        remote(part.at[pl.ds(lax.rem(z + e, NZ) * share, share)], from_z.at[e - 1], Z + e - 1, z_peer(e))
        for e in range(1, NZ)
    ]
    for copy in to_z:
        copy.start()
    for i in range(3, 5):
        update(i)
    for copy in to_z:
        copy.wait_recv()
    mine = part[pl.ds(pl.multiple_of(z * share, share), share), :]
    for e in range(NZ - 1):
        mine = mine + from_z[e]

    def stretch(xx, zz=None):
        if zz is None:
            return summed.at[0, pl.ds(core * half + xx * quarter, quarter)]
        return summed.at[0, pl.ds(core * half + xx * quarter + zz * share, share)]

    summed[0, pl.ds(pl.multiple_of(core * half + x * quarter + z * share, share), share), :] = mine
    out_z = [remote(stretch(x, z), stretch(x, z), ZG + e - 1, z_peer(e)) for e in range(1, NZ)]
    for copy in out_z:
        copy.start()
    for i in range(5, 7):
        update(i)
    for e in range(1, NZ):
        back = stretch(x, lax.rem(z + NZ - e, NZ))
        remote(back, back, ZG + e - 1, z_peer(e)).wait_recv()
    out_x = [remote(stretch(x), stretch(x), XG + d - 1, x_peer(d)) for d in range(1, NX)]
    for copy in out_x:
        copy.start()
    out_core = [remote(stretch(lax.rem(x + NX - d, NX)), stretch(lax.rem(x + NX - d, NX)), CG + d, other) for d in range(NX)]
    out_core[0].start()
    for i in range(7, 10):
        update(i)
    for d in range(1, NX):
        back = stretch(lax.rem(x + NX - d, NX))
        remote(back, back, XG + d - 1, x_peer(d)).wait_recv()
        out_core[d].start()
    for d in range(NX):
        back = summed.at[0, pl.ds((1 - core) * half + lax.rem(x + NX - d, NX) * quarter, quarter)]
        remote(back, back, CG + d, other).wait_recv()
    for copy in to_core + to_x[1:] + to_z + out_z + out_x + out_core:
        copy.wait_send()


def body(tokens, upstream, memory, block_lists, leader):
    count, features = tokens.shape
    columns = upstream.shape[1]
    chosen = block_lists.shape[2]
    half = chosen // 2
    quarter = half // NX
    share = quarter // NZ
    width = 512
    vmem = pl.BlockSpec(memory_space=pltpu.VMEM)
    hbm = pl.BlockSpec(memory_space=pl.ANY)
    return pl.pallas_call(
        kernel,
        out_shape=(
            jax.ShapeDtypeStruct((1, chosen, HD), F32),
            jax.ShapeDtypeStruct((1, features, columns), BF16),
        ),
        in_specs=[hbm, hbm, hbm, vmem, pl.BlockSpec(memory_space=pltpu.SMEM)],
        out_specs=(vmem, vmem),
        scratch_shapes=[
            pltpu.VMEM((count, features), BF16),
            pltpu.VMEM((count, columns), BF16),
            pltpu.VMEM((columns, count), BF16),
            pltpu.VMEM((features, columns), BF16),
            pltpu.VMEM((2, columns, width), F32),
            pltpu.VMEM((features * columns // HD, HD), F32),
            pltpu.VMEM((columns, chosen), BF16),
            pltpu.VMEM((1, chosen), I32),
            pltpu.VMEM((NX, 1, chosen), I32),
            pltpu.VMEM((NZ - 1, 1, chosen), I32),
            pltpu.VMEM((1, chosen), I32),
            pltpu.VMEM((1, chosen), I32),
            pltpu.VMEM((1, chosen), I32),
            pltpu.SMEM((1, chosen), I32),
            pltpu.VMEM((NX, quarter, HD), F32),
            pltpu.VMEM((NX, quarter, HD), F32),
            pltpu.VMEM((NX, quarter, HD), F32),
            pltpu.VMEM((NX - 1, quarter, HD), F32),
            pltpu.VMEM((NZ - 1, share, HD), F32),
            pltpu.VMEM((quarter, HD), F32),
            pltpu.SemaphoreType.DMA((1 + 2 * (features // width),)),
            pltpu.SemaphoreType.DMA,
            pltpu.SemaphoreType.DMA((39,)),
            pltpu.SemaphoreType.DMA((39,)),
        ],
        compiler_params=pltpu.CompilerParams(
            collective_id=0, has_side_effects=True, vmem_limit_bytes=48 * 2**20
        ),
        name="scalecom",
    )(tokens, upstream, memory, block_lists[0], leader)


def solution(mesh):
    placed = (
        P("dp", None),
        P("dp", "tensor"),
        P("dp", None, "tensor"),
        P("dp", "tensor", None),
        P(),
    )
    return jax.shard_map(
        body,
        mesh=mesh,
        in_specs=placed,
        out_specs=(P("tensor", None, None), P("dp", None, "tensor")),
        check_vma=False,
    )
```

time: 252 us -> 55.5 us (0.22)
  waiting for transfers between devices: 104 us -> 0 us
  blocking collectives: 75.4 us -> 0 us
  Pallas kernels: 0 us -> 46.9 us
  local copies, waits for them, and re-layouts: 33.9 us -> 7.13 us
  between operations: 14.9 us -> 1.3 us
  matrix products: 13.3 us -> 0 us
  other arithmetic: 9.75 us -> 0 us
    reduce_scatter x1 -> x0, waiting for transfers between devices: 104 us -> none  [body(): owned = lax.psum_scatter(packed, 'dp', scatter_dimension=0, tiled=True)]
    all_gather x1 -> x0, blocking collectives: 54.7 us -> none  [body(): summed = lax.all_gather(owned, 'dp', axis=0, tiled=True)]
    pallas_call x0 -> x1, Pallas kernels: none -> 46.9 us  [body(): pl.pallas_call(kernel, out_shape=(jax.ShapeDtypeStruct((1, chosen, HD), F...]
    psum x1 -> x0, blocking collectives: 20.7 us -> none  [broadcast(): return lax.psum(kept, axis)]
    mul x4 -> x0, local copies, waits for them, and re-layouts: 15.7 us -> none  [body(): error = (blocks * unsent[:, None]).reshape(features, columns)]
    dot_general x1 -> x0, matrix products: 13.3 us -> none  [body(): lax.dot_general(tokens, upstream, (((0,), (0,)), ((), ())), preferred_ele...]
    broadcast_in_dim x1 -> x0, other arithmetic: 8.71 us -> none  [body(): return (summed[None], updated[None])]
    reshape x1 -> x0, local copies, waits for them, and re-layouts: 7.39 us -> none  [body(): blocks = (gradient + stored).reshape(features * heads_here, HD)]
  transfers between devices with their start and end apart: 1 -> 0, of which waited for: 1 -> 0; matrix products, arithmetic and copies ran while one was open for 11% -> 0% of each run, Pallas kernels for 0% -> 0%
where the time goes in v1:
time: 55.5 us; the launch traced here: 55.3 us
  Pallas kernels  46.9 us (85%)
  local copies, waits for them, and re-layouts  7.13 us (13%)
  between operations  1.3 us (2%)
    pallas_call x1, Pallas kernels, body(): pl.pallas_call(kernel, out_shape=(jax.ShapeDtypeStruct((1, chosen, HD), F...  46.9 us
    unnamed x6, local copies, waits for them, and re-layouts  7.13 us

profile of v1, /device:TPU:1, one launch (start us, length us, event | category | flops | bytes accessed | tf_op | source)
XLA Modules:
  0.0 55.3 jit_solution(15707024961407488358)
XLA Ops:
  1.3 0.0 copy-start
  1.3 1.7 %copy-done = bf16[2048,640]{1,0:T(8,128)(2,1)S(1)} copy-done((bf16[2048,640]{1,0:T(8,128)(2,1)S(1)}, bf16[2048,640]{1,0:T(8,128)(2,1)}, u32[]{:S(2)}) %copy-start) | copy-done | bytes 2621464
  3.0 0.0 copy-start.1
  3.0 0.7 %copy-done.1 = s32[1,1,1024]{2,1,0:T(1,128)S(1)} copy-done((s32[1,1,1024]{2,1,0:T(1,128)S(1)}, s32[1,1,1024]{2,1,0:T(1,128)}, u32[]{:S(2)}) %copy-start.1) | copy-done | bytes 4120
  3.7 46.9 %scalecom.1 = (f32[1,1024,128]{2,1,0:T(8,128)S(1)}, bf16[1,2560,640]{2,1,0:T(8,128)(2,1)}) custom-call(bf16[2048,2560]{1,0:T(8,128)(2,1)} %tokens.1, bf16[2048,640]{1,0:T(8,128)(2,1)S(1)} %copy-done, bf16[1,2560,640]{2,1,0:T(8,128)(2,1)} %memory.1, s32[1,1024]{1,0:T(1,128)S(1)} %bitcast.1, s32[1]{0:T(128)S(6)} %copy.9.leader), custom_call_target="tpu_custom_call" | custom-call | tf_op jit(solution)/shard_map/scalecom/pallas_call | solution.py:229
  50.6 0.8 %copy.10 = f32[1,1024,128]{2,1,0:T(8,128)} copy(f32[1,1024,128]{2,1,0:T(8,128)S(1)} %get-tuple-element.4) | data formatting | bytes 1048576
  51.4 3.9 %copy.11 = bf16[1,2560,640]{2,1,0:T(8,128)(2,1)} copy(bf16[1,2560,640]{2,1,0:T(8,128)(2,1)} %get-tuple-element.5) | data formatting | bytes 6553600
Async XLA Ops:
  1.3 1.7 %copy-start = (bf16[2048,640]{1,0:T(8,128)(2,1)S(1)}, bf16[2048,640]{1,0:T(8,128)(2,1)}, u32[]{:S(2)}) copy-start(bf16[2048,640]{1,0:T(8,128)(2,1)} %upstream.1) | copy-start | bytes 7864324
  3.0 0.7 %copy-start.1 = (s32[1,1,1024]{2,1,0:T(1,128)S(1)}, s32[1,1,1024]{2,1,0:T(1,128)}, u32[]{:S(2)}) copy-start(s32[1,1,1024]{2,1,0:T(1,128)} %param.8) | copy-start | bytes 12292

commit v2 on v1

v2 whole, which is shorter than its diff:
```python
import functools

import jax
import jax.numpy as jnp
from jax import lax
from jax.experimental import pallas as pl
from jax.experimental.pallas import tpu as pltpu
from jax.sharding import PartitionSpec as P

HD = 128
LOWPASS = 0.3
VMEM_MIB = 40
NX, NZ = 4, 8
F32, BF16, I32 = jnp.float32, jnp.bfloat16, jnp.int32
MESH = pl.DeviceIdType.MESH


def dot(a, b, ca, cb):
    return lax.dot_general(a, b, (((ca,), (cb,)), ((), ())), preferred_element_type=F32)


def far_first():
    zs = [(NZ // 2 + (j + 1) // 2 * (1 - 2 * (j % 2))) % NZ for j in range(NZ)]
    xs = [(NX // 2 + (j + 1) // 2 * (1 - 2 * (j % 2))) % NX for j in range(NX)]
    return [(dx, dz) for dz in zs for dx in xs]


def kernel(
    tokens, upstream, memory, lists, leader, summed, updated,
    tok, up, up_t, mem, grad_t, blocks, heads, own_list, lone, peer_list, all_lists, rows_at, heads_at, index_v, index_s,
    peer_part, own_part, from_core, from_chips,
    load_sem, index_sem, send_sem, recv_sem,
):
    features = tokens.shape[1]
    columns = upstream.shape[1]
    heads_here = columns // HD
    chosen = lists.shape[1]
    half, quarter, share = chosen // 2, chosen // 2 // NX, chosen // 2 // NX // NZ
    width = grad_t.shape[2]
    chunks = features // width
    slots = NX * NZ
    chips = far_first()
    away = chips[:-1]

    me = lax.axis_index("dp")
    core = lax.rem(me, 2)
    z = lax.rem(me // 2, NZ)
    x = me // (2 * NZ)
    other = {"dp": me + 1 - 2 * core}

    def chip(dx, dz):
        return {"dp": (lax.rem(x + dx, NX) * NZ + lax.rem(z + dz, NZ)) * 2 + core}

    def remote(src, dst, at, device):
        return pltpu.make_async_remote_copy(
            src_ref=src, dst_ref=dst, send_sem=send_sem.at[at], recv_sem=recv_sem.at[at],
            device_id=device, device_id_type=MESH,
        )

    pieces = 4
    in_piece = slots // pieces
    L1, L2 = 0, 1
    C = L2 + slots - 1
    R = C + pieces
    G = R + slots - 1
    F = G + slots - 1

    barrier = pltpu.get_barrier_semaphore()
    for dx, dz in away:
        pl.semaphore_signal(barrier, inc=1, device_id=chip(dx, dz), device_id_type=MESH)
    pl.semaphore_signal(barrier, inc=1, device_id=other, device_id_type=MESH)

    load_list = pltpu.make_async_copy(lists, own_list, index_sem.at[1])
    load_list.start()
    load_up = pltpu.make_async_copy(upstream, up, load_sem.at[0])
    load_up.start()
    loads = []
    for i in range(chunks):
        at = pl.ds(i * width, width)
        load = pltpu.make_async_copy(tokens.at[:, at], tok.at[:, at], load_sem.at[1 + 2 * i])
        load.start()
        keep = pltpu.make_async_copy(memory.at[0, at], mem.at[at], load_sem.at[2 + 2 * i])
        keep.start()
        loads.append((load, keep))

    load_list.wait()
    block = own_list[...]
    row = lax.shift_right_logical(block * 52429, 18)
    code = (block - row * heads_here) * 4096 + row
    lone[...] = code * jnp.where(leader[0] == me, 1, 0)

    load_up.wait()
    piece = 512
    for j in range(up.shape[0] // piece):
        up_t[:, j * piece : (j + 1) * piece] = up[j * piece : (j + 1) * piece, :].T

    def finish(i):
        grad = grad_t[i % 2].T
        stored = mem[i * width : (i + 1) * width, :].astype(F32)
        for h in range(heads_here):
            cols = slice(h * HD, (h + 1) * HD)
            blocks[pl.ds(h * features + i * width, width), :] = grad[:, cols] + stored[:, cols]

    to_peer = remote(lone, peer_list, L1, other)
    to_all = [remote(own_list, all_lists.at[s], L2 + s, chip(dx, dz)) for s, (dx, dz) in enumerate(away)]
    index_copy = pltpu.make_async_copy(index_v, index_s, index_sem.at[0])

    for i in range(chunks):
        if i == 2:
            pl.semaphore_wait(barrier, slots)
            to_peer.start()
            to_peer.wait()
            own_list[...] = lone[...] + peer_list[...]
            for copy in to_all:
                copy.start()
        for load in loads[i]:
            load.wait()
        grad_t[i % 2] = dot(up_t[...], tok[:, i * width : (i + 1) * width], 1, 0)
        if i > 0:
            finish(i - 1)
    finish(chunks - 1)

    for copy in to_all:
        copy.wait_recv()
    total = own_list[...]
    for s in range(slots - 1):
        total = total + all_lists[s]
    head = lax.shift_right_logical(total, 12)
    row = total - head * 4096
    rows_at[...] = row
    heads_at[...] = head
    index_v[...] = head * features + row
    index_copy.start()
    index_copy.wait()

    def bent(j, n):
        return lax.rem(n // 2 + (j + 1) // 2 * (1 - 2 * lax.rem(j, 2)), n)

    def gather(target, piece, first_row):
        @pl.loop(0, in_piece)
        def _(step):
            slot = piece * in_piece + step
            to_x = lax.rem(x + bent(lax.rem(slot, NX), NX), NX)
            to_z = lax.rem(z + bent(slot // NX, NZ), NZ)
            start = first_row + (to_x * NZ + to_z) * share
            base = pl.multiple_of(slot * share, share)
            for u in range(share):
                at = index_s[0, start + u]
                target[pl.ds(base + u, 1), :] = blocks[pl.ds(at, 1), :]

    to_core = []
    for p in range(pieces):
        gather(peer_part, p, (1 - core) * half)
        rows = pl.ds(p * quarter, quarter)
        copy = remote(peer_part.at[rows], from_core.at[rows], C + p, other)
        copy.start()
        to_core.append(copy)
    to_chips = []
    for p in range(pieces):
        gather(own_part, p, core * half)
        to_core[p].wait_recv()
        rows = slice(p * quarter, (p + 1) * quarter)
        own_part[rows, :] = own_part[rows, :] + from_core[rows, :]
        for s in range(p * in_piece, min((p + 1) * in_piece, slots - 1)):
            copy = remote(own_part.at[pl.ds(s * share, share)], from_chips.at[s], R + s, chip(*chips[s]))
            copy.start()
            to_chips.append(copy)

    head_row = lax.broadcasted_iota(I32, (columns, 1), 0) // HD
    heads[...] = jnp.where(head_row == heads_at[...], 1.0, 0.0).astype(BF16)

    size = 256

    def update(i):
        at = slice(i * size, (i + 1) * size)
        feature = lax.broadcasted_iota(I32, (size, 1), 0) + i * size
        hit = jnp.where(feature == rows_at[...], 1.0, 0.0).astype(BF16)
        unsent = 1.0 - dot(hit, heads[...], 1, 1)
        for h in range(heads_here):
            cols = slice(h * HD, (h + 1) * HD)
            error = blocks[pl.ds(h * features + i * size, size), :] * unsent[:, cols]
            stored = mem[at, cols].astype(F32)
            updated[0, at, cols] = ((1.0 - LOWPASS) * stored + LOWPASS * error).astype(BF16)

    for i in range(0, 8):
        update(i)

    for copy in to_chips:
        copy.wait_recv()
    mine = own_part[(slots - 1) * share : slots * share, :]
    for s in range(slots - 1):
        mine = mine + from_chips[s]

    def share_of(xx, zz):
        return summed.at[0, pl.ds(core * half + xx * quarter + zz * share, share)]

    def quarter_of(cc, xx):
        return summed.at[0, pl.ds(cc * half + xx * quarter, quarter)]

    summed[0, pl.ds(pl.multiple_of(core * half + x * quarter + z * share, share), share), :] = mine
    out = [remote(share_of(x, z), share_of(x, z), G + s, chip(dx, dz)) for s, (dx, dz) in enumerate(away)]
    for copy in out:
        copy.start()
    for i in range(8, features // size):
        update(i)
    to_other = []
    for dx in (0, 1, NX - 1, 2):
        from_x = lax.rem(x + NX - dx, NX)
        for s, (sx, sz) in enumerate(away):
            if sx == dx:
                back = share_of(from_x, lax.rem(z + NZ - sz, NZ))
                remote(back, back, G + s, chip(sx, sz)).wait_recv()
        copy = remote(quarter_of(core, from_x), quarter_of(core, from_x), F + dx, other)
        copy.start()
        to_other.append(copy)
    for dx in (0, 1, NX - 1, 2):
        back = quarter_of(1 - core, lax.rem(x + NX - dx, NX))
        remote(back, back, F + dx, other).wait_recv()
    for copy in to_all + to_core + to_chips + out + to_other:
        copy.wait_send()


def body(tokens, upstream, memory, block_lists, leader):
    count, features = tokens.shape
    columns = upstream.shape[1]
    chosen = block_lists.shape[2]
    half = chosen // 2
    quarter = half // NX
    share = quarter // NZ
    width = 512
    hbm = pl.BlockSpec(memory_space=pltpu.HBM)
    vmem = pl.BlockSpec(memory_space=pltpu.VMEM)
    copies = 3 * (NX * NZ - 1) + 9
    summed, updated = pl.pallas_call(
        kernel,
        out_shape=(
            pltpu.VMEM((1, chosen, HD), F32),
            pltpu.VMEM((1, features, columns), BF16),
        ),
        in_specs=[hbm, hbm, hbm, hbm, pl.BlockSpec(memory_space=pltpu.SMEM)],
        out_specs=(vmem, vmem),
        scratch_shapes=[
            pltpu.VMEM((count, features), BF16),
            pltpu.VMEM((count, columns), BF16),
            pltpu.VMEM((columns, count), BF16),
            pltpu.VMEM((features, columns), BF16),
            pltpu.VMEM((2, columns, width), F32),
            pltpu.VMEM((features * columns // HD, HD), F32),
            pltpu.VMEM((columns, chosen), BF16),
            pltpu.VMEM((1, chosen), I32),
            pltpu.VMEM((1, chosen), I32),
            pltpu.VMEM((1, chosen), I32),
            pltpu.VMEM((NX * NZ - 1, 1, chosen), I32),
            pltpu.VMEM((1, chosen), I32),
            pltpu.VMEM((1, chosen), I32),
            pltpu.VMEM((1, chosen), I32),
            pltpu.SMEM((1, chosen), I32),
            pltpu.VMEM((half, HD), F32),
            pltpu.VMEM((half, HD), F32),
            pltpu.VMEM((half, HD), F32),
            pltpu.VMEM((NX * NZ - 1, share, HD), F32),
            pltpu.SemaphoreType.DMA((1 + 2 * (features // width),)),
            pltpu.SemaphoreType.DMA((2,)),
            pltpu.SemaphoreType.DMA((copies,)),
            pltpu.SemaphoreType.DMA((copies,)),
        ],
        compiler_params=pltpu.CompilerParams(
            collective_id=0, has_side_effects=True, vmem_limit_bytes=VMEM_MIB * 2**20
        ),
        name="scalecom",
    )(*(pltpu.with_memory_space_constraint(a, pltpu.HBM) for a in (tokens, upstream, memory, block_lists[0])), leader)
    return summed, updated


def solution(mesh):
    placed = (
        P("dp", None),
        P("dp", "tensor"),
        P("dp", None, "tensor"),
        P("dp", "tensor", None),
        P(),
    )
    return jax.shard_map(
        body,
        mesh=mesh,
        in_specs=placed,
        out_specs=(P("tensor", None, None), P("dp", None, "tensor")),
        check_vma=False,
    )
```

time: 55.5 us -> 51.1 us (0.921)
  local copies, waits for them, and re-layouts: 7.13 us -> 2.5 us
    unnamed x6 -> x2, local copies, waits for them, and re-layouts: 7.13 us -> 2.5 us
where the time goes in v2:
time: 51.1 us; the launch traced here: 51 us
  Pallas kernels  47.2 us (92%)
  local copies, waits for them, and re-layouts  2.5 us (5%)
  between operations  1.29 us (3%)
    pallas_call x1, Pallas kernels, body(): pl.pallas_call(kernel, out_shape=(pltpu.VMEM((1, chosen, HD), F32), pltpu...  47.2 us
    unnamed x2, local copies, waits for them, and re-layouts  2.5 us

profile of v2, /device:TPU:1, one launch (start us, length us, event | category | flops | bytes accessed | tf_op | source)
XLA Modules:
  0.0 51.0 jit_solution(17405874881813436928)
XLA Ops:
  1.3 47.2 %scalecom.1 = (f32[1,1024,128]{2,1,0:T(8,128)S(1)}, bf16[1,2560,640]{2,1,0:T(8,128)(2,1)S(1)}) custom-call(bf16[2048,2560]{1,0:T(8,128)(2,1)} %tokens.1, bf16[2048,640]{1,0:T(8,128)(2,1)} %upstream.1, bf16[1,2560,640]{2,1,0:T(8,128)(2,1)} %memory.1, s32[1,1024]{1,0:T(1,128)} %bitcast.1, s32[1]{0:T(128)S(6)} %copy.11.leader), custom_call_target="tpu_custom_call" | custom-call | tf_op jit(solution)/shard_map/scalecom/pallas_call | solution.py:234
  48.5 0.8 %copy.9 = f32[1,1024,128]{2,1,0:T(8,128)} copy(f32[1,1024,128]{2,1,0:T(8,128)S(1)} %get-tuple-element.2) | data formatting | bytes 1048576
  49.3 1.7 %copy.10 = bf16[1,2560,640]{2,1,0:T(8,128)(2,1)} copy(bf16[1,2560,640]{2,1,0:T(8,128)(2,1)S(1)} %get-tuple-element.3) | data formatting | bytes 6553600

commit v3 on v2

--- a/solution.py
+++ b/solution.py
@@ -10,6 +10,11 @@
 HD = 128
 LOWPASS = 0.3
 VMEM_MIB = 40
+SIZES = (512, 512, 512, 512, 512)
+LIST_AT = 1
+ORDER = (0, 1, 4, 2, 5, 3, 6, 7)
+UPDATES = (8, 2)
+STAGGER = ()
 NX, NZ = 4, 8
 F32, BF16, I32 = jnp.float32, jnp.bfloat16, jnp.int32
 MESH = pl.DeviceIdType.MESH
@@ -27,7 +32,7 @@
 
 def kernel(
     tokens, upstream, memory, lists, leader, summed, updated,
-    tok, up, up_t, mem, grad_t, blocks, heads, own_list, lone, peer_list, all_lists, rows_at, heads_at, index_v, index_s,
+    tok, up, mem, blocks, heads, own_list, lone, peer_list, all_lists, rows_at, heads_at, index_v, index_s,
     peer_part, own_part, from_core, from_chips,
     load_sem, index_sem, send_sem, recv_sem,
 ):
@@ -36,8 +41,8 @@
     heads_here = columns // HD
     chosen = lists.shape[1]
     half, quarter, share = chosen // 2, chosen // 2 // NX, chosen // 2 // NX // NZ
-    width = grad_t.shape[2]
-    chunks = features // width
+    offsets = [sum(SIZES[:i]) for i in range(len(SIZES))]
+    chunks = len(SIZES)
     slots = NX * NZ
     chips = far_first()
     away = chips[:-1]
@@ -74,14 +79,14 @@
     load_list.start()
     load_up = pltpu.make_async_copy(upstream, up, load_sem.at[0])
     load_up.start()
-    loads = []
+    loads, keeps = [], []
     for i in range(chunks):
-        at = pl.ds(i * width, width)
-        load = pltpu.make_async_copy(tokens.at[:, at], tok.at[:, at], load_sem.at[1 + 2 * i])
-        load.start()
-        keep = pltpu.make_async_copy(memory.at[0, at], mem.at[at], load_sem.at[2 + 2 * i])
-        keep.start()
-        loads.append((load, keep))
+        at = pl.ds(offsets[i], SIZES[i])
+        loads.append(pltpu.make_async_copy(tokens.at[:, at], tok.at[:, at], load_sem.at[1 + 2 * i]))
+        keeps.append(pltpu.make_async_copy(memory.at[0, at], mem.at[at], load_sem.at[2 + 2 * i]))
+
+    loads[0].start()
+    keeps[0].start()
 
     load_list.wait()
     block = own_list[...]
@@ -89,36 +94,30 @@
     code = (block - row * heads_here) * 4096 + row
     lone[...] = code * jnp.where(leader[0] == me, 1, 0)
 
-    load_up.wait()
-    piece = 512
-    for j in range(up.shape[0] // piece):
-        up_t[:, j * piece : (j + 1) * piece] = up[j * piece : (j + 1) * piece, :].T
-
-    def finish(i):
-        grad = grad_t[i % 2].T
-        stored = mem[i * width : (i + 1) * width, :].astype(F32)
-        for h in range(heads_here):
-            cols = slice(h * HD, (h + 1) * HD)
-            blocks[pl.ds(h * features + i * width, width), :] = grad[:, cols] + stored[:, cols]
-
     to_peer = remote(lone, peer_list, L1, other)
     to_all = [remote(own_list, all_lists.at[s], L2 + s, chip(dx, dz)) for s, (dx, dz) in enumerate(away)]
     index_copy = pltpu.make_async_copy(index_v, index_s, index_sem.at[0])
 
     for i in range(chunks):
-        if i == 2:
+        if i == LIST_AT:
             pl.semaphore_wait(barrier, slots)
             to_peer.start()
             to_peer.wait()
             own_list[...] = lone[...] + peer_list[...]
             for copy in to_all:
                 copy.start()
-        for load in loads[i]:
-            load.wait()
-        grad_t[i % 2] = dot(up_t[...], tok[:, i * width : (i + 1) * width], 1, 0)
-        if i > 0:
-            finish(i - 1)
-    finish(chunks - 1)
+        if i == 0:
+            load_up.wait()
+        loads[i].wait()
+        keeps[i].wait()
+        if i + 1 < chunks:
+            loads[i + 1].start()
+            keeps[i + 1].start()
+        at = slice(offsets[i], offsets[i] + SIZES[i])
+        grad = dot(tok[:, at], up[...], 0, 0)
+        for h in range(heads_here):
+            cols = slice(h * HD, (h + 1) * HD)
+            blocks[pl.ds(h * features + offsets[i], SIZES[i]), :] = grad[:, cols] + mem[at, cols].astype(F32)
 
     for copy in to_all:
         copy.wait_recv()
@@ -134,29 +133,31 @@
     index_copy.wait()
 
     def bent(j, n):
-        return lax.rem(n // 2 + (j + 1) // 2 * (1 - 2 * lax.rem(j, 2)), n)
+        return (n // 2 + ((j + 1) >> 1) * (1 - 2 * (j & 1))) & (n - 1)
 
     def gather(target, piece, first_row):
         @pl.loop(0, in_piece)
         def _(step):
             slot = piece * in_piece + step
-            to_x = lax.rem(x + bent(lax.rem(slot, NX), NX), NX)
-            to_z = lax.rem(z + bent(slot // NX, NZ), NZ)
+            to_x = (x + bent(slot & (NX - 1), NX)) & (NX - 1)
+            to_z = (z + bent(slot >> 2, NZ)) & (NZ - 1)
             start = first_row + (to_x * NZ + to_z) * share
             base = pl.multiple_of(slot * share, share)
+            found = [blocks[pl.ds(index_s[0, start + u], 1), :] for u in range(share)]
             for u in range(share):
-                at = index_s[0, start + u]
-                target[pl.ds(base + u, 1), :] = blocks[pl.ds(at, 1), :]
-
-    to_core = []
-    for p in range(pieces):
-        gather(peer_part, p, (1 - core) * half)
-        rows = pl.ds(p * quarter, quarter)
-        copy = remote(peer_part.at[rows], from_core.at[rows], C + p, other)
-        copy.start()
-        to_core.append(copy)
+                target[pl.ds(base + u, 1), :] = found[u]
+
+    to_core = [
+        remote(peer_part.at[pl.ds(p * quarter, quarter)], from_core.at[pl.ds(p * quarter, quarter)], C + p, other)
+        for p in range(pieces)
+    ]
     to_chips = []
-    for p in range(pieces):
+    for turn in ORDER:
+        p = turn % pieces
+        if turn < pieces:
+            gather(peer_part, p, (1 - core) * half)
+            to_core[p].start()
+            continue
         gather(own_part, p, core * half)
         to_core[p].wait_recv()
         rows = slice(p * quarter, (p + 1) * quarter)
@@ -182,7 +183,7 @@
             stored = mem[at, cols].astype(F32)
             updated[0, at, cols] = ((1.0 - LOWPASS) * stored + LOWPASS * error).astype(BF16)
 
-    for i in range(0, 8):
+    for i in range(0, UPDATES[0]):
         update(i)
 
     for copy in to_chips:
@@ -199,9 +200,13 @@
 
     summed[0, pl.ds(pl.multiple_of(core * half + x * quarter + z * share, share), share), :] = mine
     out = [remote(share_of(x, z), share_of(x, z), G + s, chip(dx, dz)) for s, (dx, dz) in enumerate(away)]
-    for copy in out:
+    done = UPDATES[0]
+    for s, copy in enumerate(out):
         copy.start()
-    for i in range(8, features // size):
+        if s in STAGGER:
+            update(done)
+            done += 1
+    for i in range(done, features // size):
         update(i)
     to_other = []
     for dx in (0, 1, NX - 1, 2):
@@ -220,6 +225,17 @@
         copy.wait_send()
 
 
+def flush(summed, updated, summed_out, updated_out, sem):
+    copies = [
+        pltpu.make_async_copy(updated, updated_out, sem.at[0]),
+        pltpu.make_async_copy(summed, summed_out, sem.at[1]),
+    ]
+    for copy in copies:
+        copy.start()
+    for copy in copies:
+        copy.wait()
+
+
 def body(tokens, upstream, memory, block_lists, leader):
     count, features = tokens.shape
     columns = upstream.shape[1]
@@ -227,7 +243,6 @@
     half = chosen // 2
     quarter = half // NX
     share = quarter // NZ
-    width = 512
     hbm = pl.BlockSpec(memory_space=pltpu.HBM)
     vmem = pl.BlockSpec(memory_space=pltpu.VMEM)
     copies = 3 * (NX * NZ - 1) + 9
@@ -242,9 +257,7 @@
         scratch_shapes=[
             pltpu.VMEM((count, features), BF16),
             pltpu.VMEM((count, columns), BF16),
-            pltpu.VMEM((columns, count), BF16),
             pltpu.VMEM((features, columns), BF16),
-            pltpu.VMEM((2, columns, width), F32),
             pltpu.VMEM((features * columns // HD, HD), F32),
             pltpu.VMEM((columns, chosen), BF16),
             pltpu.VMEM((1, chosen), I32),
@@ -259,7 +272,7 @@
             pltpu.VMEM((half, HD), F32),
             pltpu.VMEM((half, HD), F32),
             pltpu.VMEM((NX * NZ - 1, share, HD), F32),
-            pltpu.SemaphoreType.DMA((1 + 2 * (features // width),)),
+            pltpu.SemaphoreType.DMA((1 + 2 * len(SIZES),)),
             pltpu.SemaphoreType.DMA((2,)),
             pltpu.SemaphoreType.DMA((copies,)),
             pltpu.SemaphoreType.DMA((copies,)),
@@ -269,7 +282,17 @@
         ),
         name="scalecom",
     )(*(pltpu.with_memory_space_constraint(a, pltpu.HBM) for a in (tokens, upstream, memory, block_lists[0])), leader)
-    return summed, updated
+    return pl.pallas_call(
+        flush,
+        out_shape=(
+            jax.ShapeDtypeStruct(summed.shape, F32),
+            jax.ShapeDtypeStruct(updated.shape, BF16),
+        ),
+        in_specs=[vmem, vmem],
+        out_specs=(hbm, hbm),
+        scratch_shapes=[pltpu.SemaphoreType.DMA((2,))],
+        name="flush",
+    )(summed, updated)
 
 
 def solution(mesh):

time: 51.1 us -> 51.2 us (level)
    pallas_call x1, Pallas kernels: 47.2 us -> 43.1 us  [body(): pl.pallas_call(kernel, out_shape=(pltpu.VMEM((1, chosen, HD), F32), pltpu...]
    pallas_call x0 -> x1, Pallas kernels: none -> 3.98 us  [body(): pl.pallas_call(flush, out_shape=(jax.ShapeDtypeStruct(summed.shape, F32),...]
    unnamed x2 -> x4, local copies, waits for them, and re-layouts: 2.5 us -> 2.47 us
where the time goes in v3:
time: 51.2 us; the launch traced here: 51 us
  Pallas kernels  47.1 us (92%)
  local copies, waits for them, and re-layouts  2.47 us (5%)
  between operations  1.46 us (3%)
    pallas_call x1, Pallas kernels, body(): pl.pallas_call(kernel, out_shape=(pltpu.VMEM((1, chosen, HD), F32), pltpu...  43.1 us
    pallas_call x1, Pallas kernels, body(): pl.pallas_call(flush, out_shape=(jax.ShapeDtypeStruct(summed.shape, F32),...  3.98 us
    unnamed x4, local copies, waits for them, and re-layouts  2.47 us

profile of v3, /device:TPU:1, one launch (start us, length us, event | category | flops | bytes accessed | tf_op | source)
XLA Modules:
  0.0 51.0 jit_solution(2949440587634105146)
XLA Ops:
  1.3 43.1 %scalecom.1 = (f32[1,1024,128]{2,1,0:T(8,128)S(1)}, bf16[1,2560,640]{2,1,0:T(8,128)(2,1)S(1)}) custom-call(bf16[2048,2560]{1,0:T(8,128)(2,1)} %tokens.1, bf16[2048,640]{1,0:T(8,128)(2,1)} %upstream.1, bf16[1,2560,640]{2,1,0:T(8,128)(2,1)} %memory.1, s32[1,1024]{1,0:T(1,128)} %bitcast.1, s32[1]{0:T(128)S(6)} %copy.7.leader), custom_call_target="tpu_custom_call" | custom-call | tf_op jit(solution)/shard_map/scalecom/pallas_call | solution.py:249
  44.4 0.0 copy-start
  44.4 1.7 %copy-done = bf16[1,2560,640]{2,1,0:T(8,128)(2,1)} copy-done((bf16[1,2560,640]{2,1,0:T(8,128)(2,1)}, bf16[1,2560,640]{2,1,0:T(8,128)(2,1)S(1)}, u32[]{:S(2)}) %copy-start) | copy-done | bytes 3276824
  46.1 0.0 copy-start.1
  46.1 0.8 %copy-done.1 = f32[1,1024,128]{2,1,0:T(8,128)} copy-done((f32[1,1024,128]{2,1,0:T(8,128)}, f32[1,1024,128]{2,1,0:T(8,128)S(1)}, u32[]{:S(2)}) %copy-start.1) | copy-done | bytes 524312
  46.9 4.0 %flush.1 = (f32[1,1024,128]{2,1,0:T(8,128)}, bf16[1,2560,640]{2,1,0:T(8,128)(2,1)}) custom-call(f32[1,1024,128]{2,1,0:T(8,128)} %copy-done.1, bf16[1,2560,640]{2,1,0:T(8,128)(2,1)} %copy-done), custom_call_target="tpu_custom_call" | custom-call | tf_op jit(solution)/shard_map/flush/pallas_call | solution.py:285
Async XLA Ops:
  44.4 1.7 %copy-start = (bf16[1,2560,640]{2,1,0:T(8,128)(2,1)}, bf16[1,2560,640]{2,1,0:T(8,128)(2,1)S(1)}, u32[]{:S(2)}) copy-start(bf16[1,2560,640]{2,1,0:T(8,128)(2,1)S(1)} %get-tuple-element.5.updated) | copy-start | bytes 9830404
  46.1 0.8 %copy-start.1 = (f32[1,1024,128]{2,1,0:T(8,128)}, f32[1,1024,128]{2,1,0:T(8,128)S(1)}, u32[]{:S(2)}) copy-start(f32[1,1024,128]{2,1,0:T(8,128)S(1)} %get-tuple-element.4.summed) | copy-start | bytes 1572868

commit v4 on v3

--- a/solution.py
+++ b/solution.py
@@ -291,8 +291,9 @@
         in_specs=[vmem, vmem],
         out_specs=(hbm, hbm),
         scratch_shapes=[pltpu.SemaphoreType.DMA((2,))],
+        compiler_params=pltpu.CompilerParams(vmem_limit_bytes=2**20),
         name="flush",
-    )(summed, updated)
+    )(*(pltpu.with_memory_space_constraint(a, pltpu.VMEM) for a in (summed, updated)))
 
 
 def solution(mesh):

time: 51.2 us -> 46.6 us (0.910)
  local copies, waits for them, and re-layouts: 2.47 us -> 0 us
  Pallas kernels: 47.1 us -> 45 us
    unnamed x4 -> x0, local copies, waits for them, and re-layouts: 2.47 us -> none
    pallas_call x1, Pallas kernels: 3.98 us -> 1.89 us  [body(): pl.pallas_call(flush, out_shape=(jax.ShapeDtypeStruct(summed.shape, F32),...]
where the time goes in v4:
time: 46.6 us; the launch traced here: 46.5 us
  Pallas kernels  45 us (97%)
  between operations  1.45 us (3%)
    pallas_call x1, Pallas kernels, body(): pl.pallas_call(kernel, out_shape=(pltpu.VMEM((1, chosen, HD), F32), pltpu...  43.1 us
    pallas_call x1, Pallas kernels, body(): pl.pallas_call(flush, out_shape=(jax.ShapeDtypeStruct(summed.shape, F32),...  1.89 us

profile of v4, /device:TPU:1, one launch (start us, length us, event | category | flops | bytes accessed | tf_op | source)
XLA Modules:
  0.0 46.5 jit_solution(18334478308662117277)
XLA Ops:
  1.3 43.1 %scalecom.1 = (f32[1,1024,128]{2,1,0:T(8,128)S(1)}, bf16[1,2560,640]{2,1,0:T(8,128)(2,1)S(1)}) custom-call(bf16[2048,2560]{1,0:T(8,128)(2,1)} %tokens.1, bf16[2048,640]{1,0:T(8,128)(2,1)} %upstream.1, bf16[1,2560,640]{2,1,0:T(8,128)(2,1)} %memory.1, s32[1,1024]{1,0:T(1,128)} %bitcast.1, s32[1]{0:T(128)S(6)} %copy.7.leader), custom_call_target="tpu_custom_call" | custom-call | tf_op jit(solution)/shard_map/scalecom/pallas_call | solution.py:249
  44.4 1.9 %flush.1 = (f32[1,1024,128]{2,1,0:T(8,128)}, bf16[1,2560,640]{2,1,0:T(8,128)(2,1)}) custom-call(f32[1,1024,128]{2,1,0:T(8,128)S(1)} %get-tuple-element.4.summed, bf16[1,2560,640]{2,1,0:T(8,128)(2,1)S(1)} %get-tuple-element.5.updated), custom_call_target="tpu_custom_call" | custom-call | tf_op jit(solution)/shard_map/flush/pallas_call | solution.py:285

commit v5 on v4

--- a/solution.py
+++ b/solution.py
@@ -13,7 +13,7 @@
 SIZES = (512, 512, 512, 512, 512)
 LIST_AT = 1
 ORDER = (0, 1, 4, 2, 5, 3, 6, 7)
-UPDATES = (8, 2)
+UPDATES = (6, 4)
 STAGGER = ()
 NX, NZ = 4, 8
 F32, BF16, I32 = jnp.float32, jnp.bfloat16, jnp.int32
@@ -71,10 +71,6 @@
     F = G + slots - 1
 
     barrier = pltpu.get_barrier_semaphore()
-    for dx, dz in away:
-        pl.semaphore_signal(barrier, inc=1, device_id=chip(dx, dz), device_id_type=MESH)
-    pl.semaphore_signal(barrier, inc=1, device_id=other, device_id_type=MESH)
-
     load_list = pltpu.make_async_copy(lists, own_list, index_sem.at[1])
     load_list.start()
     load_up = pltpu.make_async_copy(upstream, up, load_sem.at[0])
@@ -87,6 +83,9 @@
 
     loads[0].start()
     keeps[0].start()
+    for dx, dz in away:
+        pl.semaphore_signal(barrier, inc=1, device_id=chip(dx, dz), device_id_type=MESH)
+    pl.semaphore_signal(barrier, inc=1, device_id=other, device_id_type=MESH)
 
     load_list.wait()
     block = own_list[...]

time: 46.6 us -> 46.4 us (level)
  no operation moved by 1% of the time
where the time goes in v5:
time: 46.4 us; the launch traced here: 46.3 us
  Pallas kernels  44.9 us (97%)
  between operations  1.45 us (3%)
    pallas_call x1, Pallas kernels, body(): pl.pallas_call(kernel, out_shape=(pltpu.VMEM((1, chosen, HD), F32), pltpu...  43 us
    pallas_call x1, Pallas kernels, body(): pl.pallas_call(flush, out_shape=(jax.ShapeDtypeStruct(summed.shape, F32),...  1.89 us

profile of v5, /device:TPU:1, one launch (start us, length us, event | category | flops | bytes accessed | tf_op | source)
XLA Modules:
  0.0 46.3 jit_solution(9432709697886473913)
XLA Ops:
  1.3 43.0 %scalecom.1 = (f32[1,1024,128]{2,1,0:T(8,128)S(1)}, bf16[1,2560,640]{2,1,0:T(8,128)(2,1)S(1)}) custom-call(bf16[2048,2560]{1,0:T(8,128)(2,1)} %tokens.1, bf16[2048,640]{1,0:T(8,128)(2,1)} %upstream.1, bf16[1,2560,640]{2,1,0:T(8,128)(2,1)} %memory.1, s32[1,1024]{1,0:T(1,128)} %bitcast.1, s32[1]{0:T(128)S(6)} %copy.7.leader), custom_call_target="tpu_custom_call" | custom-call | tf_op jit(solution)/shard_map/scalecom/pallas_call | solution.py:248
  44.3 1.9 %flush.1 = (f32[1,1024,128]{2,1,0:T(8,128)}, bf16[1,2560,640]{2,1,0:T(8,128)(2,1)}) custom-call(f32[1,1024,128]{2,1,0:T(8,128)S(1)} %get-tuple-element.4.summed, bf16[1,2560,640]{2,1,0:T(8,128)(2,1)S(1)} %get-tuple-element.5.updated), custom_call_target="tpu_custom_call" | custom-call | tf_op jit(solution)/shard_map/flush/pallas_call | solution.py:284

commit v6 on v5

--- a/solution.py
+++ b/solution.py
@@ -135,7 +135,7 @@
         return (n // 2 + ((j + 1) >> 1) * (1 - 2 * (j & 1))) & (n - 1)
 
     def gather(target, piece, first_row):
-        @pl.loop(0, in_piece)
+        @pl.loop(0, in_piece, unroll=2)
         def _(step):
             slot = piece * in_piece + step
             to_x = (x + bent(slot & (NX - 1), NX)) & (NX - 1)

time: 46.4 us -> 46.4 us (level)
  no operation moved by 1% of the time
where the time goes in v6:
time: 46.4 us; the launch traced here: 46.3 us
  Pallas kernels  44.8 us (97%)
  between operations  1.45 us (3%)
    pallas_call x1, Pallas kernels, body(): pl.pallas_call(kernel, out_shape=(pltpu.VMEM((1, chosen, HD), F32), pltpu...  42.9 us
    pallas_call x1, Pallas kernels, body(): pl.pallas_call(flush, out_shape=(jax.ShapeDtypeStruct(summed.shape, F32),...  1.89 us

profile of v6, /device:TPU:1, one launch (start us, length us, event | category | flops | bytes accessed | tf_op | source)
XLA Modules:
  0.0 46.3 jit_solution(7429655949984370040)
XLA Ops:
  1.3 42.9 %scalecom.1 = (f32[1,1024,128]{2,1,0:T(8,128)S(1)}, bf16[1,2560,640]{2,1,0:T(8,128)(2,1)S(1)}) custom-call(bf16[2048,2560]{1,0:T(8,128)(2,1)} %tokens.1, bf16[2048,640]{1,0:T(8,128)(2,1)} %upstream.1, bf16[1,2560,640]{2,1,0:T(8,128)(2,1)} %memory.1, s32[1,1024]{1,0:T(1,128)} %bitcast.1, s32[1]{0:T(128)S(6)} %copy.7.leader), custom_call_target="tpu_custom_call" | custom-call | tf_op jit(solution)/shard_map/scalecom/pallas_call | solution.py:248
  44.2 1.9 %flush.1 = (f32[1,1024,128]{2,1,0:T(8,128)}, bf16[1,2560,640]{2,1,0:T(8,128)(2,1)}) custom-call(f32[1,1024,128]{2,1,0:T(8,128)S(1)} %get-tuple-element.4.summed, bf16[1,2560,640]{2,1,0:T(8,128)(2,1)S(1)} %get-tuple-element.5.updated), custom_call_target="tpu_custom_call" | custom-call | tf_op jit(solution)/shard_map/flush/pallas_call | solution.py:284
